TPU v7x, 128 devices: a whole 4x4x4 slice. The times are simulated.
128 devices in a mesh: dp: 8 (over z, core), seq: 16 (over x, y).
Axes of the slice: x: 4, y: 4, z: 4, core: 2. Of those that a mesh axis runs over, the one named last changes fastest.
Arguments:
- queries: bfloat16 [16, 16, 512, 1536], P('dp', 'seq'), may hold values from -18 to 18
- key_rows: bfloat16 [16, 16, 512, 1536], P('dp', 'seq'), may hold values from -4 to 4
- value_rows: bfloat16 [16, 16, 512, 1536], P('dp', 'seq'), may hold values from -6 to 6
- cotangent: bfloat16 [16, 16, 512, 1536], P('dp', 'seq'), may hold values from -6 to 6
- frame_counts: int32 [16], replicated, may hold values from 9 to 16
- patch_rows: int32 [16], replicated, may hold values from 10 to 16
- patch_cols: int32 [16], replicated, may hold values from 20 to 32
- swap_flags: int32 [4, 2], replicated, may hold values from 0 to 1, as said below
Outputs:
- block_out: bfloat16 [16, 16, 512, 1536], P('dp', 'seq')
- grad_queries: bfloat16 [16, 16, 512, 1536], P('dp', 'seq')
- grad_keys: bfloat16 [16, 16, 512, 1536], P('dp', 'seq')
- grad_values: bfloat16 [16, 16, 512, 1536], P('dp', 'seq')
Inputs may be any that keep to these rules, and one draw needn't show every extreme that they name: `swap_flags`: in every draw some clip is traded and some clip is not.
All inputs are finite; a program needn't handle non-finite values.
Results may differ from a plain program's by a relative error of at most 0.0058.
Values may be sent and summed in bfloat16 or wider, within the bound.
A program may use at most 256 MiB of HBM per device.

v0:
```python
import jax
import jax.numpy as jnp
from jax import lax
from jax.sharding import PartitionSpec as P

HEADS = 12
HEAD_DIM = 128
GRID_W = 32


masked_score = -1e30
spatial_forms = ("lhe,mhe->hlm", "hlm,mhe->lhe", "hlm,lhe->mhe")
temporal_forms = ("slbhe,smbhe->sbhlm", "sbhlm,smbhe->slbhe", "sbhlm,slbhe->smbhe")


def swapped(value, axis, distance):
    mask = 2**distance
    pairs = [(source, source ^ mask) for source in range(lax.axis_size(axis))]
    return lax.ppermute(value, axis, pairs)


def attention(queries, key_rows, value_rows, cotangent, key_mask, row_mask, einsum_forms):
    score_form, mix_form, back_form = einsum_forms
    scale = HEAD_DIM ** (-0.5)
    scores = jnp.einsum(score_form, queries, key_rows, preferred_element_type=jnp.float32) * scale
    scores = jnp.where(key_mask, scores, masked_score)
    row_max = jnp.max(scores, axis=-1, keepdims=True)
    exponent = jnp.exp(scores - row_max)
    softmax = exponent / jnp.sum(exponent, axis=-1, keepdims=True)
    weights = softmax.astype(jnp.bfloat16)
    masked_grad = jnp.where(row_mask, cotangent, jnp.zeros_like(cotangent))
    attended = jnp.einsum(mix_form, weights, value_rows, preferred_element_type=jnp.float32)
    grad_value = jnp.einsum(back_form, weights, masked_grad, preferred_element_type=jnp.float32)
    grad_weight = jnp.einsum(
        score_form, masked_grad, value_rows, preferred_element_type=jnp.float32
    )
    row_dot = jnp.sum(softmax * grad_weight, axis=-1, keepdims=True)
    grad_score = (softmax * (grad_weight - row_dot) * scale).astype(jnp.bfloat16)
    grad_query = jnp.einsum(mix_form, grad_score, key_rows, preferred_element_type=jnp.float32)
    grad_key = jnp.einsum(back_form, grad_score, queries, preferred_element_type=jnp.float32)
    attended = jnp.where(row_mask, attended, jnp.zeros_like(attended))
    return (attended, grad_query, grad_key, grad_value)


def pick(table_rows, clip_ids):
    match = clip_ids[:, None] == jnp.arange(table_rows.shape[0])[None, :]
    return jnp.sum(jnp.where(match, table_rows[None, :], 0), axis=1)


def replace_slots(stacked, arrived, slot_mask):
    return jnp.where(slot_mask[:, None, None, None], arrived, stacked)


def run_block(
    queries, key_rows, value_rows, cotangent, clip_ids, frame_counts, patch_rows, patch_cols
):
    slot_count, frames_dev, cell_count, width_all = queries.shape
    counts = pick(frame_counts, clip_ids)
    rows_seen = pick(patch_rows, clip_ids)
    cols_seen = pick(patch_cols, clip_ids)
    seq_count = lax.axis_size("seq")
    seq_index = lax.axis_index("seq")
    frame_ids = seq_index * frames_dev + jnp.arange(frames_dev)
    cell_ids = jnp.arange(cell_count)
    inside_cells = ((cell_ids // GRID_W)[None, :] < rows_seen[:, None]) & (
        (cell_ids % GRID_W)[None, :] < cols_seen[:, None]
    )
    inside = (frame_ids[None, :, None] < counts[:, None, None]) & inside_cells[:, None, :]
    split_shape = (slot_count * frames_dev, cell_count, HEADS, HEAD_DIM)

    def one_frame(frame_items):
        frame_query, frame_keys, frame_values, frame_grad, frame_inside = frame_items
        return attention(
            frame_query,
            frame_keys,
            frame_values,
            frame_grad,
            frame_inside[None, None, :],
            frame_inside[:, None, None],
            spatial_forms,
        )

    spatial_part = lax.map(
        one_frame,
        (
            queries.reshape(split_shape),
            key_rows.reshape(split_shape),
            value_rows.reshape(split_shape),
            cotangent.reshape(split_shape),
            inside.reshape(slot_count * frames_dev, cell_count),
        ),
    )
    regrouped = (
        lax.all_to_all(queries, "seq", split_axis=2, concat_axis=1, tiled=True),
        lax.all_to_all(key_rows, "seq", split_axis=2, concat_axis=1, tiled=True),
        lax.all_to_all(value_rows, "seq", split_axis=2, concat_axis=1, tiled=True),
        lax.all_to_all(cotangent, "seq", split_axis=2, concat_axis=1, tiled=True),
    )
    cells_dev = cell_count // seq_count
    frame_total = frames_dev * seq_count
    block_shape = (slot_count, frame_total, cells_dev, HEADS, HEAD_DIM)
    own_cells = seq_index * cells_dev + jnp.arange(cells_dev)
    inside_own = ((own_cells // GRID_W)[None, :] < rows_seen[:, None]) & (
        (own_cells % GRID_W)[None, :] < cols_seen[:, None]
    )
    inside_time = (jnp.arange(frame_total)[None, :, None] < counts[:, None, None]) & inside_own[
        :, None, :
    ]
    temporal_part = attention(
        regrouped[0].reshape(block_shape),
        regrouped[1].reshape(block_shape),
        regrouped[2].reshape(block_shape),
        regrouped[3].reshape(block_shape),
        jnp.transpose(inside_time, (0, 2, 1))[:, :, None, None, :],
        inside_time[:, :, :, None, None],
        temporal_forms,
    )
    flat_shape = (slot_count, frame_total, cells_dev, width_all)
    rounded = [tensor.astype(jnp.bfloat16).reshape(flat_shape) for tensor in temporal_part]
    returned = (
        lax.all_to_all(rounded[0], "seq", split_axis=1, concat_axis=2, tiled=True),
        lax.all_to_all(rounded[1], "seq", split_axis=1, concat_axis=2, tiled=True),
        lax.all_to_all(rounded[2], "seq", split_axis=1, concat_axis=2, tiled=True),
        lax.all_to_all(rounded[3], "seq", split_axis=1, concat_axis=2, tiled=True),
    )
    results = []
    for spatial_piece, temporal_piece in zip(spatial_part, returned):
        summed = spatial_piece.reshape(
            slot_count, frames_dev, cell_count, width_all
        ) + temporal_piece.astype(jnp.float32)
        results.append(summed.astype(jnp.bfloat16))
    return tuple(results)


def shards(
    queries, key_rows, value_rows, cotangent, frame_counts, patch_rows, patch_cols, swap_flags
):
    slot_count = queries.shape[0]
    pair_count = swap_flags.shape[0]
    group_index = lax.axis_index("dp")
    pair_bit = lax.axis_size("dp").bit_length() - 2
    own_pair = (jnp.arange(pair_count) == group_index % pair_count)[:, None]
    slot_mask = jnp.sum(jnp.where(own_pair, swap_flags, 0), axis=0) == 1
    slot_ids = jnp.arange(slot_count)
    home_ids = group_index * slot_count + slot_ids
    arrived = swapped(cotangent, "dp", pair_bit)
    home_results = run_block(
        queries,
        key_rows,
        value_rows,
        replace_slots(cotangent, arrived, slot_mask),
        home_ids,
        frame_counts,
        patch_rows,
        patch_cols,
    )
    leaving = swapped(
        (home_results[0], home_results[1], home_results[2], home_results[3]), "dp", pair_bit
    )
    results = (
        replace_slots(home_results[0], leaving[0], slot_mask),
        replace_slots(home_results[1], leaving[1], slot_mask),
        replace_slots(home_results[2], leaving[2], slot_mask),
        replace_slots(home_results[3], leaving[3], slot_mask),
    )
    return (results[0], results[1], results[2], results[3])


def solution(mesh):
    return jax.shard_map(
        shards,
        mesh=mesh,
        in_specs=(
            P("dp", "seq", None, None),
            P("dp", "seq", None, None),
            P("dp", "seq", None, None),
            P("dp", "seq", None, None),
            P(),
            P(),
            P(),
            P(),
        ),
        out_specs=(
            P("dp", "seq", None, None),
            P("dp", "seq", None, None),
            P("dp", "seq", None, None),
            P("dp", "seq", None, None),
        ),
        check_vma=False,
    )
```

profile of v0, /device:TPU:36, one launch (start us, length us, event | category | flops | bytes accessed | tf_op | source)
XLA Modules:
  0.0 797.3 jit_solution(11357870863932542931)
XLA Ops:
  0.6 6.8 copy.223
  7.4 7.5 all-to-all-start.1
  14.9 6.8 copy.221
  21.7 34.0 %all-to-all-done.1 = bf16[2,1,512,1536]{3,0,1,2:T(2,128)(2,1)S(1)} async-done(((bf16[2,1,512,1536]{3,0,1,2:T(2,128)(2,1)}), bf16[2,1,512,1536]{3,0,1,2:T(2,128)(2,1)S(1)}, u32[]{:S(2)}, u32[]{:S(2)}) %all-to-all-start.1) | async-done | bytes 3145760 | tf_op jit(solution)/shard_map/all_to_all | solution.py:95
  55.6 9.6 %all-to-all-start = ((bf16[2,1,512,1536]{3,0,1,2:T(2,128)(2,1)}), bf16[2,1,512,1536]{3,0,1,2:T(2,128)(2,1)}, u32[]{:S(2)}, u32[]{:S(2)}) async-start(bf16[2,1,512,1536]{3,0,1,2:T(2,128)(2,1)} %copy.221), calls=%async_computation | async-start | bytes 6291456 | tf_op jit(solution)/shard_map/all_to_all | solution.py:94
  65.2 4.6 copy.217
  72.9 6.8 copy.227
  79.7 24.6 %all-to-all-done = bf16[2,1,512,1536]{3,0,1,2:T(2,128)(2,1)} async-done(((bf16[2,1,512,1536]{3,0,1,2:T(2,128)(2,1)}), bf16[2,1,512,1536]{3,0,1,2:T(2,128)(2,1)}, u32[]{:S(2)}, u32[]{:S(2)}) %all-to-all-start) | async-done | bytes 3145760 | tf_op jit(solution)/shard_map/all_to_all | solution.py:94
  104.3 7.0 all-to-all-start.2
  111.9 27.8 %collective-permute-done = bf16[2,1,512,1536]{2,3,0,1:T(8,128)(2,1)} collective-permute-done((bf16[2,1,512,1536]{2,3,0,1:T(8,128)(2,1)}, bf16[2,1,512,1536]{2,3,0,1:T(8,128)(2,1)}, u32[]{:S(2)}, u32[]{:S(2)}) %collective-permute-start) | collective-permute-done | bytes 3145760 | tf_op jit(solution)/shard_map/ppermute | solution.py:19
  142.9 5.8 copy.235
  148.6 7.2 all-to-all-start.4
  156.1 8.8 %reshape.423 = bf16[2,16,32,12,128]{4,3,0,2,1:T(8,128)(2,1)} reshape(bf16[2,1,512,1536]{3,0,1,2:T(2,128)(2,1)} %copy-done.2) | data formatting | bytes 6291456 | tf_op jit(solution)/shard_map/reshape | solution.py:111
  164.9 8.8 %reshape.422 = bf16[2,16,32,12,128]{4,3,0,2,1:T(8,128)(2,1)} reshape(bf16[2,1,512,1536]{3,0,1,2:T(2,128)(2,1)} %all-to-all-done) | data formatting | bytes 6291456 | tf_op jit(solution)/shard_map/reshape | solution.py:110
  173.7 8.8 %reshape.424 = bf16[2,16,32,12,128]{4,3,0,2,1:T(8,128)(2,1)} reshape(bf16[2,1,512,1536]{3,0,1,2:T(2,128)(2,1)} %all-to-all-done.2) | data formatting | bytes 6291456 | tf_op jit(solution)/shard_map/reshape | solution.py:112
  182.5 7.2 fusion.85
  189.7 5.2 fusion.109
  194.9 5.0 fusion.62
  203.0 6.9 reshape.417
  209.9 17.2 %all-to-all-start.3 = ((bf16[2,16,32,1536]{3,2,0,1:T(8,128)(2,1)}), bf16[2,16,32,1536]{3,2,0,1:T(8,128)(2,1)}, u32[]{:S(2)}, u32[]{:S(2)}) async-start(bf16[2,16,32,1536]{3,2,0,1:T(8,128)(2,1)} %reshape.417), calls=%async_computation.3 | async-start | bytes 6291456 | tf_op jit(solution)/shard_map/all_to_all | solution.py:121
  227.1 8.8 %reshape.418 = bf16[2,16,32,12,128]{4,3,0,2,1:T(8,128)(2,1)} reshape(bf16[2,1,512,1536]{3,0,1,2:T(2,128)(2,1)} %all-to-all-done.4) | data formatting | bytes 6291456 | tf_op jit(solution)/shard_map/reshape | solution.py:113
  235.9 6.6 convert_bitcast_fusion
  245.6 6.9 reshape.421
  252.4 10.4 %all-to-all-done.3 = bf16[2,16,32,1536]{3,2,0,1:T(8,128)(2,1)} async-done(((bf16[2,16,32,1536]{3,2,0,1:T(8,128)(2,1)}), bf16[2,16,32,1536]{3,2,0,1:T(8,128)(2,1)}, u32[]{:S(2)}, u32[]{:S(2)}) %all-to-all-start.3) | async-done | bytes 3145760 | tf_op jit(solution)/shard_map/all_to_all | solution.py:121
  262.8 8.4 %all-to-all-start.7 = ((bf16[2,16,32,1536]{3,2,0,1:T(8,128)(2,1)}), bf16[2,16,32,1536]{3,2,0,1:T(8,128)(2,1)}, u32[]{:S(2)}, u32[]{:S(2)}) async-start(bf16[2,16,32,1536]{3,2,0,1:T(8,128)(2,1)} %reshape.421), calls=%async_computation.7 | async-start | bytes 6291456 | tf_op jit(solution)/shard_map/all_to_all | solution.py:124
  271.3 4.6 copy.214
  275.9 4.6 copy.215
  280.6 4.6 copy.216
  285.3 10.0 %fusion.81 = f32[2,32,12,16,16]{3,4,2,1,0:T(8,128)} fusion(bf16[2,16,32,12,128]{4,3,0,2,1:T(8,128)(2,1)} %reshape.424, bf16[2,16,32,12,128]{4,3,0,2,1:T(8,128)(2,1)} %reshape.418, pred[2,16,32]{1,2,0:T(8,128)(4,1)S(1)} %broadcast_and_fusion.1), kind=kOutput, calls=%fused_computation.91 | convolution fusion | flops 51904512 | bytes 7078912 | tf_op jit(solution)/shard_map/slbhe,smbhe->sbhlm/dot_general | solution.py:34
  295.3 14.5 %convert_bitcast_fusion.2 = bf16[2,16,32,12,128]{4,1,3,2,0:T(8,128)(2,1)} fusion(f32[2,32,12,16,16]{3,4,2,1,0:T(8,128)} %fusion.81, bf16[2,16,32,12,128]{4,3,0,2,1:T(8,128)(2,1)} %reshape.423, f32[2,32,12,16,16]{3,4,2,1,0:T(8,128)} %get-tuple-element.173, f32[2,32,12,16]{3,2,1,0:T(8,128)} %copy-done.9), kind=kOutput, calls=%fused_computation.79 | convolution fusion | flops 53293072 | bytes 7913472 | tf_op jit(solution)/shard_map/sbhlm,smbhe->slbhe/dot_general | solution.py:39
  309.8 4.9 copy.271
  314.7 6.9 reshape.419
  321.6 7.2 all-to-all-start.5
  328.8 150.4 %while.16 = (s32[]{:T(128)}, f32[2,512,12,128]{1,3,2,0:T(8,128)}, f32[2,512,12,128]{1,3,2,0:T(8,128)}, f32[2,512,12,128]{1,3,2,0:T(8,128)}, f32[2,512,12,128]{1,...) while((s32[]{:T(128)}, f32[2,512,12,128]{1,3,2,0:T(8,128)}, ...), condition=%wide.region_8.9_spmd, body=%wide.region_4.8_spmd.sunk | while | flops 4909708800 | bytes 214131888 | solution.py:83
  333.0 9.2 %fusion.134 = (f32[12,512]{1,0:T(8,128)S(1)}, f32[12,512,512]{1,2,0:T(8,128)}) fusion(f32[12,512,512]{1,2,0:T(8,128)S(1)} %fusion.133, pred[512]{0:T(512)(128)(4,1)S(1)} %dynamic-slice_reduce_fusion.2), kind=kOutput, calls=%fused_computation.142.clone.1 | output fusion | flops 18874880 | bytes 25190912 | tf_op jit(solution)/shard_map/while/body/eval_jaxpr/sub | solution.py:28
  342.2 7.8 bitcast_dynamic-update-slice_fusion.8
  350.0 6.3 fusion.135
  356.3 19.7 %bitcast_dynamic-update-slice_fusion.9 = f32[2,512,12,128]{1,3,2,0:T(8,128)} fusion(f32[2,512,12,128]{1,3,2,0:T(8,128)} %get-tuple-element.256, s32[]{:T(128)S(6)} %copy.310, f32[12,512,512]{1,2,0:T(8,128)} %fusion.135, bf16[2,512,12,128]{1,3,2,0:T(8,128)(2,1)} %get-tuple-element.273, f32[12,512,512]{1,2,0:T(8,128)} %get-tuple-element.241, ...), kind=kOutput, calls=%fused_computation.16.clone.1 | convolution fusion | flops 827333120 | bytes 55116800 | tf_op jit(solution)/shard_map/while/body/eval_jaxpr/hlm,mhe->lhe/dot_general | solution.py:39
  376.0 19.7 %bitcast_dynamic-update-slice_fusion.10 = f32[2,512,12,128]{1,3,2,0:T(8,128)} fusion(f32[2,512,12,128]{1,3,2,0:T(8,128)} %get-tuple-element.257, s32[]{:T(128)S(6)} %copy.310, f32[12,512,512]{1,2,0:T(8,128)} %fusion.135, bf16[2,512,12,128]{1,3,2,0:T(8,128)(2,1)} %get-tuple-element.272, f32[12,512,512]{1,2,0:T(8,128)} %get-tuple-element.241, ...), kind=kOutput, calls=%fused_computation.15.clone.1 | convolution fusion | flops 827333120 | bytes 55116800 | tf_op jit(solution)/shard_map/while/body/eval_jaxpr/hlm,lhe->mhe/dot_general | solution.py:40
  395.7 8.5 %bitcast_dynamic-update-slice_fusion.11 = f32[2,512,12,128]{1,3,2,0:T(8,128)} fusion(f32[2,512,12,128]{1,3,2,0:T(8,128)} %get-tuple-element.258, s32[]{:T(128)S(6)} %copy.310, bf16[2,512,12,128]{1,3,2,0:T(8,128)(2,1)S(1)} %get-tuple-element.274, pred[512]{0:T(512)(128)(4,1)S(1)} %dynamic-slice_reduce_fusion.2, ...), kind=kOutput, calls=%fused_computation.14.clone.1 | convolution fusion | flops 812384256 | bytes 17335808 | tf_op jit(solution)/shard_map/while/body/eval_jaxpr/hlm,lhe->mhe/dot_general | solution.py:33
  407.9 9.2 %fusion.134 = (f32[12,512]{1,0:T(8,128)S(1)}, f32[12,512,512]{1,2,0:T(8,128)}) fusion(f32[12,512,512]{1,2,0:T(8,128)S(1)} %fusion.133, pred[512]{0:T(512)(128)(4,1)S(1)} %dynamic-slice_reduce_fusion.2), kind=kOutput, calls=%fused_computation.142.clone.1 | output fusion | flops 18874880 | bytes 25190912 | tf_op jit(solution)/shard_map/while/body/eval_jaxpr/sub | solution.py:28
  417.1 7.9 bitcast_dynamic-update-slice_fusion.8
  425.1 6.3 fusion.135
  431.4 19.7 %bitcast_dynamic-update-slice_fusion.9 = f32[2,512,12,128]{1,3,2,0:T(8,128)} fusion(f32[2,512,12,128]{1,3,2,0:T(8,128)} %get-tuple-element.256, s32[]{:T(128)S(6)} %copy.310, f32[12,512,512]{1,2,0:T(8,128)} %fusion.135, bf16[2,512,12,128]{1,3,2,0:T(8,128)(2,1)} %get-tuple-element.273, f32[12,512,512]{1,2,0:T(8,128)} %get-tuple-element.241, ...), kind=kOutput, calls=%fused_computation.16.clone.1 | convolution fusion | flops 827333120 | bytes 55116800 | tf_op jit(solution)/shard_map/while/body/eval_jaxpr/hlm,mhe->lhe/dot_general | solution.py:39
  451.1 19.6 %bitcast_dynamic-update-slice_fusion.10 = f32[2,512,12,128]{1,3,2,0:T(8,128)} fusion(f32[2,512,12,128]{1,3,2,0:T(8,128)} %get-tuple-element.257, s32[]{:T(128)S(6)} %copy.310, f32[12,512,512]{1,2,0:T(8,128)} %fusion.135, bf16[2,512,12,128]{1,3,2,0:T(8,128)(2,1)} %get-tuple-element.272, f32[12,512,512]{1,2,0:T(8,128)} %get-tuple-element.241, ...), kind=kOutput, calls=%fused_computation.15.clone.1 | convolution fusion | flops 827333120 | bytes 55116800 | tf_op jit(solution)/shard_map/while/body/eval_jaxpr/hlm,lhe->mhe/dot_general | solution.py:40
  470.7 8.4 %bitcast_dynamic-update-slice_fusion.11 = f32[2,512,12,128]{1,3,2,0:T(8,128)} fusion(f32[2,512,12,128]{1,3,2,0:T(8,128)} %get-tuple-element.258, s32[]{:T(128)S(6)} %copy.310, bf16[2,512,12,128]{1,3,2,0:T(8,128)(2,1)S(1)} %get-tuple-element.274, pred[512]{0:T(512)(128)(4,1)S(1)} %dynamic-slice_reduce_fusion.2, ...), kind=kOutput, calls=%fused_computation.14.clone.1 | convolution fusion | flops 812384256 | bytes 17335808 | tf_op jit(solution)/shard_map/while/body/eval_jaxpr/hlm,lhe->mhe/dot_general | solution.py:33
  485.2 6.6 copy.234
  491.8 7.4 fusion.63
  502.1 13.0 %convert_bitcast_fusion.1 = bf16[2,16,32,12,128]{4,1,3,2,0:T(8,128)(2,1)S(1)} fusion(f32[2,32,12,16,16]{3,4,2,1,0:T(8,128)} %fusion.81, bf16[2,16,32,12,128]{4,3,0,2,1:T(8,128)(2,1)} %reshape.422, f32[2,32,12,16,16]{3,4,2,1,0:T(8,128)} %get-tuple-element.173, f32[2,32,12,16]{3,2,1,0:T(8,128)} %copy-done.9), kind=kOutput, calls=%fused_computation.78 | convolution fusion | flops 53293072 | bytes 7913472 | tf_op jit(solution)/shard_map/sbhlm,slbhe->smbhe/dot_general | solution.py:40
  518.2 6.9 reshape.420
  528.9 7.2 all-to-all-start.6
  536.2 5.4 bitcast_convert_fusion
  541.6 6.6 copy.253
  548.2 7.4 fusion.59
  562.1 6.6 copy.244
  568.7 7.4 fusion.61
  583.2 6.6 copy.249
  589.8 5.7 fusion.60
  596.1 43.3 %collective-permute-done.4 = bf16[2,1,512,1536]{2,3,0,1:T(8,128)(2,1)} collective-permute-done((bf16[2,1,512,1536]{2,3,0,1:T(8,128)(2,1)}, bf16[2,1,512,1536]{2,3,0,1:T(8,128)(2,1)}, u32[]{:S(2)}, u32[]{:S(2)}) %collective-permute-start.4) | collective-permute-done | bytes 3145760 | tf_op jit(solution)/shard_map/ppermute | solution.py:19
  639.4 67.4 %collective-permute-done.2 = bf16[2,1,512,1536]{2,3,0,1:T(8,128)(2,1)} collective-permute-done((bf16[2,1,512,1536]{2,3,0,1:T(8,128)(2,1)}, bf16[2,1,512,1536]{2,3,0,1:T(8,128)(2,1)}, u32[]{:S(2)}, u32[]{:S(2)}) %collective-permute-start.2) | collective-permute-done | bytes 3145760 | tf_op jit(solution)/shard_map/ppermute | solution.py:19
  706.8 62.7 %collective-permute-done.3 = bf16[2,1,512,1536]{2,3,0,1:T(8,128)(2,1)S(1)} collective-permute-done((bf16[2,1,512,1536]{2,3,0,1:T(8,128)(2,1)S(1)}, bf16[2,1,512,1536]{2,3,0,1:T(8,128)(2,1)S(1)}, u32[]{:S(2)}, u32[]{:S(2)}) %collective-permute-start.3) | collective-permute-done | bytes 3145760 | tf_op jit(solution)/shard_map/ppermute | solution.py:19
  769.6 10.9 %broadcast_select_fusion = (bf16[2,1,512,1536]{2,3,0,1:T(8,128)(2,1)S(1)}, bf16[2,1,512,1536]{2,3,0,1:T(8,128)(2,1)}, bf16[2,1,512,1536]{2,3,0,1:T(8,128)(2,1)}, bf16[2,1,512,1536]{2,3,0,1:T(8,128)(2,1)}) fusion(bf16[2,1,512,1536]{2,3,0,1:T(8,128)(2,1)} %collective-permute-done.4, bf16[2,1,512,1536]{2,3,0,1:T(8,128)(2,1)} %fusion.59, ...), kind=kLoop, calls=%fused_computation.83 | loop fusion | flops 6291456 | bytes 37748736 | tf_op jit(solution)/shard_map/jit(_where)/select_n | solution.py:51
  780.4 4.6 copy.254
  785.1 4.6 copy.255
  (67 shorter events, 58.3 us)
Async XLA Ops:
  7.4 48.2 %all-to-all-start.1 = ((bf16[2,1,512,1536]{3,0,1,2:T(2,128)(2,1)}), bf16[2,1,512,1536]{3,0,1,2:T(2,128)(2,1)S(1)}, u32[]{:S(2)}, u32[]{:S(2)}) async-start(bf16[2,1,512,1536]{3,0,1,2:T(2,128)(2,1)} %copy.223), calls=%async_computation.1 | async-start | bytes 6291456 | tf_op jit(solution)/shard_map/all_to_all | solution.py:95
  55.6 14.2 %copy-start.2 = (bf16[2,1,512,1536]{3,0,1,2:T(2,128)(2,1)}, bf16[2,1,512,1536]{3,0,1,2:T(2,128)(2,1)S(1)}, u32[]{:S(2)}) copy-start(bf16[2,1,512,1536]{3,0,1,2:T(2,128)(2,1)S(1)} %all-to-all-done.1) | copy-start | bytes 9437188
  55.6 48.7 %all-to-all-start = ((bf16[2,1,512,1536]{3,0,1,2:T(2,128)(2,1)}), bf16[2,1,512,1536]{3,0,1,2:T(2,128)(2,1)}, u32[]{:S(2)}, u32[]{:S(2)}) async-start(bf16[2,1,512,1536]{3,0,1,2:T(2,128)(2,1)} %copy.221), calls=%async_computation | async-start | bytes 6291456 | tf_op jit(solution)/shard_map/all_to_all | solution.py:94
  69.8 41.6 %copy-start.5 = (s32[4,2]{0,1:T(2,128)S(1)}, s32[4,2]{0,1:T(2,128)}, u32[]{:S(2)}) copy-start(s32[4,2]{0,1:T(2,128)} %param.17) | copy-start | bytes 100
  69.8 41.7 %copy-start.6 = (s32[16]{0:T(128)S(1)}, s32[16]{0:T(128)}, u32[]{:S(2)}) copy-start(s32[16]{0:T(128)} %param.14) | copy-start | bytes 196
  69.9 41.7 %copy-start.7 = (s32[16]{0:T(128)S(1)}, s32[16]{0:T(128)}, u32[]{:S(2)}) copy-start(s32[16]{0:T(128)} %param.16) | copy-start | bytes 196
  69.9 41.7 %copy-start.8 = (s32[16]{0:T(128)S(1)}, s32[16]{0:T(128)}, u32[]{:S(2)}) copy-start(s32[16]{0:T(128)} %param.15) | copy-start | bytes 196
  69.9 69.7 %collective-permute-start = (bf16[2,1,512,1536]{2,3,0,1:T(8,128)(2,1)}, bf16[2,1,512,1536]{2,3,0,1:T(8,128)(2,1)}, u32[]{:S(2)}, u32[]{:S(2)}) collective-permute-start(bf16[2,1,512,1536]{2,3,0,1:T(8,128)(2,1)} %copy.217), channel_id=1, source_target_pairs={{0,64},{16,80},{32,96},{48,112},{64,0},{80,16},{96,32},{112,48},{1... | collective-permute-start | bytes 9437192 | tf_op jit(solution)/shard_map/ppermute | solution.py:19
  104.3 44.3 %all-to-all-start.2 = ((bf16[2,1,512,1536]{3,0,1,2:T(2,128)(2,1)}), bf16[2,1,512,1536]{3,0,1,2:T(2,128)(2,1)}, u32[]{:S(2)}, u32[]{:S(2)}) async-start(bf16[2,1,512,1536]{3,0,1,2:T(2,128)(2,1)} %copy.227), calls=%async_computation.2 | async-start | bytes 6291456 | tf_op jit(solution)/shard_map/all_to_all | solution.py:96
  111.8 36.9 %copy-start.3 = (pred[2]{0:T(512)(128)(4,1)}, pred[2]{0:T(512)(128)(4,1)S(1)}, u32[]{:S(2)}) copy-start(pred[2]{0:T(512)(128)(4,1)S(1)} %broadcast_compare_fusion.1) | copy-start | bytes 10
  148.6 61.3 %all-to-all-start.4 = ((bf16[2,1,512,1536]{3,0,1,2:T(2,128)(2,1)}), bf16[2,1,512,1536]{3,0,1,2:T(2,128)(2,1)}, u32[]{:S(2)}, u32[]{:S(2)}) async-start(bf16[2,1,512,1536]{3,0,1,2:T(2,128)(2,1)} %copy.235), calls=%async_computation.4 | async-start | bytes 6291456 | tf_op jit(solution)/shard_map/all_to_all | solution.py:97
  189.7 5.2 copy-start.1
  194.9 5.0 copy-start.9
  209.9 52.9 %all-to-all-start.3 = ((bf16[2,16,32,1536]{3,2,0,1:T(8,128)(2,1)}), bf16[2,16,32,1536]{3,2,0,1:T(8,128)(2,1)}, u32[]{:S(2)}, u32[]{:S(2)}) async-start(bf16[2,16,32,1536]{3,2,0,1:T(8,128)(2,1)} %reshape.417), calls=%async_computation.3 | async-start | bytes 6291456 | tf_op jit(solution)/shard_map/all_to_all | solution.py:121
  262.8 58.8 %all-to-all-start.7 = ((bf16[2,16,32,1536]{3,2,0,1:T(8,128)(2,1)}), bf16[2,16,32,1536]{3,2,0,1:T(8,128)(2,1)}, u32[]{:S(2)}, u32[]{:S(2)}) async-start(bf16[2,16,32,1536]{3,2,0,1:T(8,128)(2,1)} %reshape.421), calls=%async_computation.7 | async-start | bytes 6291456 | tf_op jit(solution)/shard_map/all_to_all | solution.py:124
  321.6 207.3 %all-to-all-start.5 = ((bf16[2,16,32,1536]{3,2,0,1:T(8,128)(2,1)}), bf16[2,16,32,1536]{3,2,0,1:T(8,128)(2,1)}, u32[]{:S(2)}, u32[]{:S(2)}) async-start(bf16[2,16,32,1536]{3,2,0,1:T(8,128)(2,1)} %reshape.419), calls=%async_computation.5 | async-start | bytes 6291456 | tf_op jit(solution)/shard_map/all_to_all | solution.py:122
  342.2 7.9 copy-start
  417.1 7.9 copy-start
  499.1 97.0 %collective-permute-start.1 = (bf16[2,1,512,1536]{2,3,0,1:T(8,128)(2,1)}, bf16[2,1,512,1536]{2,3,0,1:T(8,128)(2,1)}, u32[]{:S(2)}, u32[]{:S(2)}) collective-permute-start(bf16[2,1,512,1536]{2,3,0,1:T(8,128)(2,1)} %fusion.63), channel_id=1, source_target_pairs={{0,64},{16,80},{32,96},{48,112},{64,0},{80,16},{96,32},{112,48},{1... | collective-permute-start | bytes 9437192 | tf_op jit(solution)/shard_map/ppermute | solution.py:19
  528.9 50.3 %all-to-all-start.6 = ((bf16[2,16,32,1536]{3,2,0,1:T(8,128)(2,1)}), bf16[2,16,32,1536]{3,2,0,1:T(8,128)(2,1)S(1)}, u32[]{:S(2)}, u32[]{:S(2)}) async-start(bf16[2,16,32,1536]{3,2,0,1:T(8,128)(2,1)} %reshape.420), calls=%async_computation.6 | async-start | bytes 6291456 | tf_op jit(solution)/shard_map/all_to_all | solution.py:123
  555.6 83.9 %collective-permute-start.4 = (bf16[2,1,512,1536]{2,3,0,1:T(8,128)(2,1)}, bf16[2,1,512,1536]{2,3,0,1:T(8,128)(2,1)}, u32[]{:S(2)}, u32[]{:S(2)}) collective-permute-start(bf16[2,1,512,1536]{2,3,0,1:T(8,128)(2,1)} %fusion.59), channel_id=1, source_target_pairs={{0,64},{16,80},{32,96},{48,112},{64,0},{80,16},{96,32},{112,48},{1... | collective-permute-start | bytes 9437192 | tf_op jit(solution)/shard_map/ppermute | solution.py:19
  576.0 130.8 %collective-permute-start.2 = (bf16[2,1,512,1536]{2,3,0,1:T(8,128)(2,1)}, bf16[2,1,512,1536]{2,3,0,1:T(8,128)(2,1)}, u32[]{:S(2)}, u32[]{:S(2)}) collective-permute-start(bf16[2,1,512,1536]{2,3,0,1:T(8,128)(2,1)} %fusion.61), channel_id=1, source_target_pairs={{0,64},{16,80},{32,96},{48,112},{64,0},{80,16},{96,32},{112,48},{1... | collective-permute-start | bytes 9437192 | tf_op jit(solution)/shard_map/ppermute | solution.py:19
  589.8 179.8 %copy-start.4 = (pred[2]{0:T(512)(128)(4,1)S(1)}, pred[2]{0:T(512)(128)(4,1)}, u32[]{:S(2)}) copy-start(pred[2]{0:T(512)(128)(4,1)} %copy-done.3) | copy-start | bytes 10
  595.5 174.1 %collective-permute-start.3 = (bf16[2,1,512,1536]{2,3,0,1:T(8,128)(2,1)S(1)}, bf16[2,1,512,1536]{2,3,0,1:T(8,128)(2,1)S(1)}, u32[]{:S(2)}, u32[]{:S(2)}) collective-permute-start(bf16[2,1,512,1536]{2,3,0,1:T(8,128)(2,1)S(1)} %fusion.60), channel_id=1, source_target_pairs={{0,64},{16,80},{32,96},{48,112},{64,0},{80,16},{96,32},{112,48},{1... | collective-permute-start | bytes 9437192 | tf_op jit(solution)/shard_map/ppermute | solution.py:19
where the time goes:
time: 805 us; the launch traced here: 797 us
  waiting for transfers between devices  270 us (34%)
  matrix products  188 us (23%)
  local copies, waits for them, and re-layouts  173 us (21%)
  other arithmetic  83 us (10%)
  starting transfers between devices  81.7 us (10%)
    ppermute x5, waiting for transfers between devices, swapped(): return lax.ppermute(value, axis, pairs)  201 us
    unnamed x29, local copies, waits for them, and re-layouts  55.6 us
    dot_general x3, matrix products, attention(): jnp.einsum(mix_form, grad_score, key_rows, preferred_element_type=jnp.flo...  53.9 us
    dot_general x3, matrix products, attention(): jnp.einsum(back_form, grad_score, queries, preferred_element_type=jnp.flo...  52.3 us
    reshape x8, local copies, waits for them, and re-layouts, run_block(): tensor.astype(jnp.bfloat16).reshape(flat_shape)  41.6 us
    all_to_all x1, waiting for transfers between devices, run_block(): lax.all_to_all(key_rows, 'seq', split_axis=2, concat_axis=1, tiled=True)  34 us
    convert_element_type x4, other arithmetic, run_block(): results.append(summed.astype(jnp.bfloat16))  27.8 us
    convert_element_type x4, local copies, waits for them, and re-layouts, run_block(): temporal_piece.astype(jnp.float32)  26.4 us
  transfers between devices with their start and end apart: 13, of which 7 were waited for; matrix products, arithmetic and copies ran while one was open for 51% of the time, Pallas kernels for 0%

commit v1 on v0

v1 whole, which is shorter than its diff:
```python
import functools

import jax
import jax.numpy as jnp
from jax import lax
from jax.experimental import pallas as pl
from jax.experimental.pallas import tpu as pltpu
from jax.sharding import PartitionSpec as P

HEAD_DIM = 128
GRID_W = 32
CELLS = 512
FRAMES = 16
SLOTS = 2
WIDTH = 1536
PACK = 2 * HEAD_DIM
CHUNKS = WIDTH // PACK
SCALE = HEAD_DIM**-0.5
LOG2E = 1.4426950408889634
MASKED = -1e30
MESH = pl.DeviceIdType.MESH
BF16 = jnp.bfloat16
F32 = jnp.float32
LAG_TIME = 1
LAG_SPACE = 2
OFFSETS = (
    (1, 0), (3, 0), (0, 1), (0, 3), (1, 1), (3, 3), (1, 3), (3, 1),
    (2, 0), (0, 2), (2, 2), (1, 2), (3, 2), (2, 1), (2, 3),
)


def dot(a, b, dims):
    return lax.dot_general(a, b, (dims, ((), ())), preferred_element_type=F32)


def attend(q, k, v, g, bias):
    s = dot(q, k, ((1,), (1,))) * (SCALE * LOG2E) + bias
    e = jnp.exp2(s - jnp.max(s, axis=-1, keepdims=True))
    p = e * (1.0 / jnp.sum(e, axis=-1, keepdims=True))
    pb = p.astype(BF16)
    o = dot(pb, v, ((1,), (0,)))
    dv = dot(pb, g, ((0,), (0,)))
    dp = dot(g, v, ((1,), (1,)))
    row_dot = jnp.sum(p * dp, axis=-1, keepdims=True)
    ds = (p * (dp - row_dot) * SCALE).astype(BF16)
    dq = dot(ds, k, ((1,), (0,)))
    dk = dot(ds, q, ((0,), (0,)))
    return o, dq, dk, dv


def block_kernel(
    n,
    q_hbm, k_hbm, v_hbm, g_hbm,
    pack_ref, unpack_ref, swap_ref, row_ref, space_bias, time_bias, diag_ref,
    o_hbm, dq_hbm, dk_hbm, dv_hbm,
    moved, own, grad, grad_out, stage, work, back, space, result,
    z_send, z_recv, own_sem, grad_sem, gs_send, f_send, f_recv, b_send, b_recv, out_sem,
):
    rows = 2 * n
    cap = 16 * n
    me = lax.axis_index("seq")
    group = lax.axis_index("dp")
    partner = lax.rem(group + 4, 8)
    mx, my = me // 4, lax.rem(me, 4)
    peers = [lax.rem(mx + ox, 4) * 4 + lax.rem(my + oy, 4) for ox, oy in OFFSETS]
    homes = (q_hbm, k_hbm, v_hbm)
    outs = (o_hbm, dq_hbm, dk_hbm, dv_hbm)

    def columns(i):
        return pl.ds(pl.multiple_of(i * PACK, PACK), PACK)

    def own_copies(i):
        return [
            pltpu.make_async_copy(
                homes[a].at[:, :, columns(i)], own.at[lax.rem(i, 2), a], own_sem.at[lax.rem(i, 2)]
            )
            for a in range(3)
        ]

    def z_copies(i):
        return [
            pltpu.make_async_remote_copy(
                src_ref=homes[a].at[:, :, columns(i)],
                dst_ref=moved.at[i, a],
                send_sem=z_send.at[i],
                recv_sem=z_recv.at[i],
                device_id={"dp": partner},
                device_id_type=MESH,
            )
            for a in range(3)
        ]

    def start(copies):
        for copy in copies:
            copy.start()

    def wait_bytes(ref, sem):
        pltpu.make_async_copy(ref, ref, sem).wait()

    def packed(values):
        taken = dot(pack_ref[...], values, ((1,), (0,)))
        parts = [taken[:, b * 128 : (b + 1) * 128].reshape(16, n, 128) for b in range(2)]
        return jnp.concatenate(parts, axis=1).astype(BF16)

    barrier = pltpu.get_barrier_semaphore()
    for peer in peers:
        pl.semaphore_signal(barrier, inc=1, device_id={"seq": peer}, device_id_type=MESH)
    pl.semaphore_signal(barrier, inc=1, device_id={"dp": partner}, device_id_type=MESH)

    def load_grad(i, _):
        pltpu.make_async_copy(g_hbm.at[:, :, columns(i)], grad.at[i], grad_sem.at[i]).start()
        return 0

    lax.fori_loop(0, CHUNKS, load_grad, 0)
    start(own_copies(0))
    start(own_copies(1))
    pl.semaphore_wait(barrier, 16)
    start(z_copies(0))
    start(z_copies(1))

    def send_grad(i, _):
        wait_bytes(grad.at[i], grad_sem.at[i])
        grad_out[i] = packed(grad[i].reshape(SLOTS * CELLS, PACK))
        for peer in peers:
            pltpu.make_async_remote_copy(
                src_ref=grad_out.at[i, peer],
                dst_ref=work.at[i, me, 3],
                send_sem=gs_send.at[i],
                recv_sem=f_recv.at[i],
                device_id={"seq": peer},
                device_id_type=MESH,
            ).start()
        work[i, me, 3] = grad_out[i, me]
        return 0

    lax.fori_loop(0, CHUNKS, send_grad, 0)

    def send_chunk(i):
        slot = lax.rem(i, 2)
        wait_bytes(own.at[slot], own_sem.at[slot])
        wait_bytes(moved.at[i], z_recv.at[i])

        @pl.when(i + 2 < CHUNKS)
        def _():
            start(z_copies(i + 2))

        @pl.when(i >= 2)
        def _():
            wait_bytes(stage.at[slot, pl.ds(0, 15)], f_send.at[slot])

        for a in range(3):
            for s in range(SLOTS):
                moved[i, a, s] = jnp.where(swap_ref[s, 0:1, :] > 0, moved[i, a, s], own[slot, a, s])
            stage[slot, :, a] = packed(moved[i, a].reshape(SLOTS * CELLS, PACK))

        @pl.when(i + 2 < CHUNKS)
        def _():
            start(own_copies(i + 2))

        for peer in peers:
            pltpu.make_async_remote_copy(
                src_ref=stage.at[slot, peer],
                dst_ref=work.at[i, me, pl.ds(0, 3)],
                send_sem=f_send.at[slot],
                recv_sem=f_recv.at[i],
                device_id={"seq": peer},
                device_id_type=MESH,
            ).start()
        work[i, me, pl.ds(0, 3)] = stage[slot, me]

    def time_chunk(i):
        wait_bytes(work.at[i, pl.ds(0, 15)], f_recv.at[i])

        def one(r, _):
            at = pl.ds(pl.multiple_of(r * 16, 16), 16)
            q, k, v, g = [work[i, :, a, at, :].reshape(256, 128) for a in range(4)]
            bias = diag_ref[...] + time_bias[r, 0:1, :]
            for a, value in enumerate(attend(q, k, v, g, bias)):
                work[i, :, a, at, :] = value.astype(BF16).reshape(16, 16, 128)
            return 0

        lax.fori_loop(0, rows // 16, one, 0)
        for peer in peers:
            pltpu.make_async_remote_copy(
                src_ref=work.at[i, peer],
                dst_ref=back.at[i, me],
                send_sem=b_send.at[i],
                recv_sem=b_recv.at[i],
                device_id={"seq": peer},
                device_id_type=MESH,
            ).start()
        back[i, me] = work[i, me]

    def space_chunk(i):
        def one(step, _):
            s, b = step // 2, lax.rem(step, 2)
            lanes = pl.ds(pl.multiple_of(b * 128, 128), 128)
            q, k, v = [moved[i, a, s, :, lanes] for a in range(3)]
            seen = row_ref[s]
            g = grad[i, s, :, lanes] * seen
            o, dq, dk, dv = attend(q, k, v, g, space_bias[s, 0:1, :])
            o = o * seen.astype(F32)
            for a, value in enumerate((o, dq, dk, dv)):
                space[a, s, :, lanes] = value
            return 0

        lax.fori_loop(0, 2 * SLOTS, one, 0)
        wait_bytes(back.at[i, pl.ds(0, 15)], b_recv.at[i])

        @pl.when(i > 0)
        def _():
            wait_bytes(result, out_sem)

        for a in range(4):
            value = back[i, :, a].astype(F32)
            parts = [value[:, b * n : (b + 1) * n].reshape(cap, 128) for b in range(2)]
            taken = dot(unpack_ref[...], jnp.concatenate(parts, axis=1).astype(BF16), ((1,), (0,)))
            summed = space[a].reshape(SLOTS * CELLS, PACK) + taken
            result[a] = summed.astype(BF16).reshape(SLOTS, CELLS, PACK)
        start(
            [
                pltpu.make_async_copy(result.at[a], outs[a].at[:, :, columns(i)], out_sem)
                for a in range(4)
            ]
        )

    def step(i, _):
        @pl.when(i < CHUNKS)
        def _():
            send_chunk(i)

        @pl.when((i >= LAG_TIME) & (i < CHUNKS + LAG_TIME))
        def _():
            time_chunk(i - LAG_TIME)

        @pl.when(i >= LAG_SPACE)
        def _():
            space_chunk(i - LAG_SPACE)

        return 0

    lax.fori_loop(0, CHUNKS + LAG_SPACE, step, 0)
    wait_bytes(result, out_sem)

    def finish(i, _):
        wait_bytes(moved.at[i], z_send.at[i])
        wait_bytes(grad_out.at[i, pl.ds(0, 15)], gs_send.at[i])
        wait_bytes(work.at[i, pl.ds(0, 15)], b_send.at[i])
        return 0

    lax.fori_loop(0, CHUNKS, finish, 0)
    for slot in range(2):
        wait_bytes(stage.at[slot, pl.ds(0, 15)], f_send.at[slot])


def pick(table, ids):
    match = ids[:, None] == jnp.arange(table.shape[0])[None, :]
    return jnp.sum(jnp.where(match, table[None, :], 0), axis=1)


def run_block(n, q, k, v, g, swaps, counts, seen_rows, seen_cols):
    rows, cap = 2 * n, 16 * n
    frame = lax.axis_index("seq")
    cells = jnp.arange(CELLS)
    y, x = cells // GRID_W, cells % GRID_W
    inside = (y[None] < seen_rows[:, None]) & (x[None] < seen_cols[:, None])
    areas = seen_rows * seen_cols
    place = y[None] * seen_cols[:, None] + x[None] + jnp.array([0, 1])[:, None] * areas[0]
    live = inside & (frame < counts)[:, None]
    place = jnp.where(live, place, -1).reshape(-1)
    pack = (jnp.arange(cap)[:, None] == place[None, :]).astype(BF16)
    unpack = (place[:, None] == jnp.arange(cap)[None, :]).astype(BF16)
    swap = jnp.broadcast_to(swaps.astype(BF16)[:, None, None], (SLOTS, 16, PACK))
    row = jnp.broadcast_to(live.astype(BF16)[:, :, None], (SLOTS, CELLS, 128))
    space_bias = jnp.where(live, 0.0, MASKED).astype(F32)
    space_bias = jnp.broadcast_to(space_bias[:, None, :], (SLOTS, 8, CELLS))
    cell = frame * n + jnp.arange(rows) % n
    cell_count = jnp.where(cell < areas[0], counts[0], counts[1])
    cell_count = jnp.where(cell < areas[0] + areas[1], cell_count, FRAMES)
    alive = jnp.arange(FRAMES)[None, :, None] < cell_count.reshape(rows // 16, 1, 16)
    time_bias = jnp.where(alive, 0.0, MASKED).astype(F32).reshape(rows // 16, 1, 256)
    time_bias = jnp.broadcast_to(time_bias, (rows // 16, 8, 256))
    token = jnp.arange(256) % 16
    diag = jnp.where(token[:, None] == token[None, :], 0.0, MASKED).astype(F32)

    shape = (SLOTS, CELLS, WIDTH)
    whole = pl.BlockSpec(memory_space=pl.ANY)
    local = pl.BlockSpec(memory_space=pltpu.VMEM)
    dma = pltpu.SemaphoreType.DMA
    outs = pl.pallas_call(
        functools.partial(block_kernel, n),
        out_shape=[jax.ShapeDtypeStruct(shape, BF16)] * 4,
        in_specs=[whole] * 4 + [local] * 7,
        out_specs=[whole] * 4,
        scratch_shapes=[
            pltpu.VMEM((CHUNKS, 3, SLOTS, CELLS, PACK), BF16),
            pltpu.VMEM((2, 3, SLOTS, CELLS, PACK), BF16),
            pltpu.VMEM((CHUNKS, SLOTS, CELLS, PACK), BF16),
            pltpu.VMEM((CHUNKS, 16, rows, 128), BF16),
            pltpu.VMEM((2, 16, 3, rows, 128), BF16),
            pltpu.VMEM((CHUNKS, 16, 4, rows, 128), BF16),
            pltpu.VMEM((CHUNKS, 16, 4, rows, 128), BF16),
            pltpu.VMEM((4, SLOTS, CELLS, PACK), F32),
            pltpu.VMEM((4, SLOTS, CELLS, PACK), BF16),
            dma((CHUNKS,)),
            dma((CHUNKS,)),
            dma((2,)),
            dma((CHUNKS,)),
            dma((CHUNKS,)),
            dma((2,)),
            dma((CHUNKS,)),
            dma((CHUNKS,)),
            dma((CHUNKS,)),
            dma,
        ],
        compiler_params=pltpu.CompilerParams(
            collective_id=n // 8, has_side_effects=True, vmem_limit_bytes=63 * 2**20
        ),
        cost_estimate=pl.CostEstimate(
            flops=2 * 10**10, bytes_accessed=24 * 2**20, transcendentals=10**7
        ),
    )(
        *[value.reshape(shape) for value in (q, k, v, g)],
        pack, unpack, swap, row, space_bias, time_bias, diag,
    )
    return tuple(value.reshape(SLOTS, 1, CELLS, WIDTH) for value in outs)


SIZES = (48, 56, 64)


def shards(q, k, v, g, frame_counts, patch_rows, patch_cols, swap_flags):
    group = lax.axis_index("dp")
    clips = jnp.arange(16)
    swapped = pick(swap_flags.reshape(-1), (clips // 2 % 4) * 2 + clips % 2) == 1
    source = jnp.where(swapped, clips ^ 8, clips)
    home = group * 2 + jnp.arange(2)
    counts, seen_rows, seen_cols = [
        pick(pick(table, source), home) for table in (frame_counts, patch_rows, patch_cols)
    ]
    swaps = pick(swapped.astype(jnp.int32), home)
    needed = jnp.max(jnp.sum(pick(patch_rows * patch_cols, source).reshape(8, 2), axis=1))
    args = (q, k, v, g, swaps, counts, seen_rows, seen_cols)
    if len(SIZES) == 1:
        return run_block(SIZES[0], *args)
    choice = sum((needed > 16 * n).astype(jnp.int32) for n in SIZES[:-1])
    return lax.switch(choice, [functools.partial(run_block, n) for n in SIZES], *args)


def solution(mesh):
    rows = P("dp", "seq", None, None)
    return jax.shard_map(
        shards,
        mesh=mesh,
        in_specs=(rows, rows, rows, rows, P(), P(), P(), P()),
        out_specs=(rows, rows, rows, rows),
        check_vma=False,
    )
```

time: 805 us -> 351 us (0.44)
  Pallas kernels: 0 us -> 320 us
  waiting for transfers between devices: 270 us -> 0 us
  matrix products: 188 us -> 0 us
  local copies, waits for them, and re-layouts: 173 us -> 17 us
  starting transfers between devices: 81.7 us -> 0 us
  other arithmetic: 83 us -> 8.81 us
    pallas_call x0 -> x1, Pallas kernels: none -> 320 us  [run_block(): pl.pallas_call(functools.partial(block_kernel, n), out_shape=[jax.ShapeDt...]
    ppermute x5 -> x0, waiting for transfers between devices: 201 us -> none  [swapped(): return lax.ppermute(value, axis, pairs)]
    dot_general x18 -> x0, matrix products: 188 us -> none  [the longest x3 53.9 us: attention(): jnp.einsum(mix_form, grad_score, key_rows, preferred_element_type=jnp.flo...]
    reshape x12 -> x1, local copies, waits for them, and re-layouts: 76.7 us -> 0.08 us  [shards(): pick(patch_rows * patch_cols, source).reshape(8, 2)]
    all_to_all x8 -> x0, starting transfers between devices: 71.3 us -> none  [the longest x1 17.2 us: run_block(): lax.all_to_all(rounded[0], 'seq', split_axis=1, concat_axis=2, tiled=True)]
    all_to_all x8 -> x0, waiting for transfers between devices: 69 us -> none  [the longest x1 34 us: run_block(): lax.all_to_all(key_rows, 'seq', split_axis=2, concat_axis=1, tiled=True)]
    unnamed x29 -> x11, local copies, waits for them, and re-layouts: 55.6 us -> 12.4 us
    convert_element_type x8 -> x4, other arithmetic: 44.5 us -> 2.63 us  [the longest x1 2.61 us: run_block(): unpack = (place[:, None] == jnp.arange(cap)[None, :]).astype(BF16)]
  transfers between devices with their start and end apart: 13 -> 0, of which waited for: 7 -> 0; matrix products, arithmetic and copies ran while one was open for 51% -> 0% of each run, Pallas kernels for 0% -> 0%
where the time goes in v1:
time: 351 us; the launch traced here: 350 us
  Pallas kernels  320 us (91%)
  local copies, waits for them, and re-layouts  17 us (5%)
  other arithmetic  8.81 us (3%)
    pallas_call x1, Pallas kernels, run_block(): pl.pallas_call(functools.partial(block_kernel, n), out_shape=[jax.ShapeDt...  320 us
    unnamed x11, local copies, waits for them, and re-layouts  12.4 us

profile of v1, /device:TPU:36, one launch (start us, length us, event | category | flops | bytes accessed | tf_op | source)
XLA Modules:
  0.0 350.3 jit_solution(825574232172991943)
XLA Ops:
  0.6 0.7 mul.104
  1.3 0.8 copy.41
  2.1 0.1 broadcast_in_dim.315
  2.2 0.1 select_reduce_fusion.4
  2.3 0.9 select_reduce_fusion
  3.2 0.2 select_reduce_fusion.5
  3.4 0.1 reshape.1133
  3.5 0.1 reduce_sum.92
  3.6 0.6 reduce_max.9
  5.6 333.1 %conditional.1 = ((bf16[2,512,1536]{2,1,0:T(8,128)(2,1)}, bf16[2,512,1536]{2,1,0:T(8,128)(2,1)}, bf16[2,512,1536]{2,1,0:T(8,128)(2,1)}, bf16[2,512,1536]{2,1,0:T(8,128)(2,1)})) conditional(s32[]{:T(128)} %clamp.3, (bf16[2,1,512,1536]{3,2,1,0:T(8,128)(2,1)}, bf16[2,1,512,1536]{3,2,1,0:T(8,128)(2,1)}, ...), branch_computations={%region_11.12_spmd, %region_12.13_spmd, %region_13.14_spmd} | conditional | flops 20004354048 | bytes 30176478 | solution.py:347
  6.0 0.6 fusion.48
  7.9 0.7 broadcast_multiply_fusion.2
  8.6 0.6 fusion.49
  9.2 2.0 select_select_fusion.2
  11.1 0.1 and.354
  11.2 0.1 broadcast_bitcast_fusion.12
  11.3 0.1 broadcast_select_fusion.2
  11.4 0.1 broadcast_bitcast_fusion.13
  11.5 0.1 lt.448
  11.6 0.7 broadcast_in_dim.290.swap_ref
  12.3 0.6 broadcast_in_dim.294.space_bias
  12.9 0.1 lt.456
  13.0 0.6 broadcast_in_dim.299.time_bias
  13.6 0.9 broadcast_in_dim.291.row_ref
  14.5 0.8 compare_select_fusion.4.diag_ref
  15.3 2.6 fusion.31
  17.9 320.4 %branch_2_fun.1 = (bf16[2,512,1536]{2,1,0:T(8,128)(2,1)}, bf16[2,512,1536]{2,1,0:T(8,128)(2,1)}, bf16[2,512,1536]{2,1,0:T(8,128)(2,1)}, bf16[2,512,1536]{2,1,0:T(8,128)(2,1)}) custom-call(bf16[2,512,1536]{2,1,0:T(8,128)(2,1)} %bitcast.106, bf16[2,512,1536]{2,1,0:T(8,128)(2,1)} %bitcast.109, bf16[2,512,1536]{2,1,0:T(8,128)(2,1)} %bitcast.112, ...), custom_call_target="tpu_custom_call" | custom-call | flops 20000000000 | bytes 25165824 | tf_op jit(solution)/shard_map/cond/branch_2_fun/pallas_call | solution.py:290
  338.6 0.0 copy-start
  338.6 3.9 %copy.85 = bf16[2,1,512,1536]{3,2,1,0:T(8,128)(2,1)} copy(bf16[2,1,512,1536]{3,2,1,0:T(8,128)(2,1)} %bitcast.85) | data formatting | bytes 6291456
  342.5 0.0 copy-done
  342.5 0.0 copy-start.1
  342.5 1.7 copy.86
  344.2 1.4 copy-done.1
  345.6 0.0 copy-start.2
  345.6 1.7 copy.87
  347.2 1.4 copy-done.2
  348.6 1.7 copy.88
  (23 shorter events, 0.1 us)
Async XLA Ops:
  338.6 3.9 %copy-start = (bf16[2,512,1536]{2,1,0:T(8,128)(2,1)S(1)}, bf16[2,512,1536]{2,1,0:T(8,128)(2,1)}, u32[]{:S(2)}) copy-start(bf16[2,512,1536]{2,1,0:T(8,128)(2,1)} %get-tuple-element.100) | copy-start | bytes 9437188
  342.5 3.0 copy-start.1
  345.6 3.0 copy-start.2

commit v2 on v1

v2 whole, which is shorter than its diff:
```python
import functools

import jax
import jax.numpy as jnp
import numpy as np
from jax import lax
from jax.experimental import pallas as pl
from jax.experimental.pallas import tpu as pltpu
from jax.sharding import PartitionSpec as P

HEAD_DIM = 128
GRID_W = 32
CELLS = 512
FRAMES = 16
SLOTS = 2
WIDTH = 1536
PACK = 2 * HEAD_DIM
CHUNKS = WIDTH // PACK
SCALE = HEAD_DIM**-0.5
LOG2E = 1.4426950408889634
MASKED = -1e30
MESH = pl.DeviceIdType.MESH
BF16 = jnp.bfloat16
F32 = jnp.float32
TIME_AT = (3, 7, 11, 15, 17, 18)
SPACE_AT = (8, 11, 14, 17, 18, 19)
OFFSETS = (
    (1, 0), (3, 0), (0, 1), (0, 3), (1, 1), (3, 3), (1, 3), (3, 1),
    (2, 0), (0, 2), (2, 2), (1, 2), (3, 2), (2, 1), (2, 3),
)


def dot(a, b, dims):
    return lax.dot_general(a, b, (dims, ((), ())), preferred_element_type=F32)


def attend(q, k, v, g, bias):
    s = dot(q, k, ((1,), (1,))) * (SCALE * LOG2E) + bias
    e = jnp.exp2(s - jnp.max(s, axis=-1, keepdims=True))
    p = e * (1.0 / jnp.sum(e, axis=-1, keepdims=True))
    pb = p.astype(BF16)
    o = dot(pb, v, ((1,), (0,)))
    dv = dot(pb, g, ((0,), (0,)))
    dp = dot(g, v, ((1,), (1,)))
    row_dot = jnp.sum(p * dp, axis=-1, keepdims=True)
    ds = (p * (dp - row_dot) * SCALE).astype(BF16)
    dq = dot(ds, k, ((1,), (0,)))
    dk = dot(ds, q, ((0,), (0,)))
    return o, dq, dk, dv


@functools.cache
def reach():
    grid = [(y, x) for y in range(10, 17) for x in range(20, 33)]
    listed = {}
    for tall, broad in grid:
        y, x = np.divmod(np.arange(tall * broad), broad)
        listed[tall, broad] = y * GRID_W + x
    met = np.zeros((SLOTS * CELLS, SLOTS * CELLS), bool)
    for cells in listed.values():
        met[np.arange(cells.size), cells] = True
    second = np.zeros((CELLS, CELLS), bool)
    second |= met[:CELLS, :CELLS]
    for offset in {tall * broad for tall, broad in grid} | {256}:
        met[offset : offset + CELLS, CELLS:] |= second
    return met


def ranks(lo, hi):
    device = np.arange(16)
    x, y = device // 4, device % 4
    width = np.where((x + y) % 2 == 0, hi, lo)
    base = np.cumsum(width) - width
    cell = np.arange(hi)[None, :]
    rank = np.where(cell < width[:, None], base[:, None] + cell, -2)
    row = np.arange(2 * hi)
    cell_of = np.where(row < 2 * lo, row % lo, lo + (row - 2 * lo) % 8)
    cell_of = np.tile(cell_of.reshape(hi // 8, 1, 16), (1, FRAMES, 1)).reshape(hi // 8, 256)
    return rank.reshape(-1).astype(np.int32), cell_of.astype(np.int32)


def spans(met):
    found = []
    for k in range(0, met.shape[1], 256):
        end = min(k + 256, met.shape[1])
        hit = np.flatnonzero(met[:, k:end].any(axis=1))
        if hit.size:
            first = int(hit[0]) // 128 * 128
            last = min(-(-int(hit[-1] + 1) // 128) * 128, met.shape[0])
            found.append((k, end, first, last))
    return found


def select(one_hot, values, found):
    height = one_hot.shape[0]
    parts = [
        (first, last, dot(one_hot[first:last, k:end], values[k:end], ((1,), (0,))))
        for k, end, first, last in found
    ]
    blocks = []
    for r in range(0, height, 128):
        top = min(r + 128, height)
        terms = [p[r - first : top - first] for first, last, p in parts if first <= r < last]
        blocks.append(functools.reduce(lambda m, n: m + n, terms))
    return jnp.concatenate(blocks, axis=0)


def block_kernel(
    lo, hi,
    q_hbm, k_hbm, v_hbm, g_hbm,
    count_ref, rows_ref, cols_ref, flag_ref, rank_col, rank_row, cell_ref,
    out_hbm, back, tally,
    own, z_out, z_in, moved, grad, grad_out, stage, work, back_in, space, result,
    pack, unpack, z_pack, z_unpack, row_ref, space_bias, time_bias, diag_ref,
    z_send, z_recv, own_sem, grad_sem, gs_send, f_send, f_recv, b_send, b_recv, back_sem, out_sem,
):
    rows = 2 * hi
    cap = 16 * hi
    z_cap = 8 * (lo + hi)
    mixed = lo != hi
    raw = hi == 64
    place = ranks(lo, hi)[0]
    met = reach()[np.maximum(place, 0)] & (place >= 0)[:, None]
    pack_spans, unpack_spans = spans(met), spans(met.T)
    z_met = reach()[:z_cap]
    z_pack_spans, z_unpack_spans = spans(z_met), spans(z_met.T)
    me = lax.axis_index("seq")
    group = lax.axis_index("dp")
    partner = lax.rem(group + 4, 8)
    mx, my = me // 4, lax.rem(me, 4)
    wide = lax.rem(mx + my, 2) == 0
    peers = [
        (lax.rem(mx + ox, 4) * 4 + lax.rem(my + oy, 4), (ox + oy) % 2 == 0) for ox, oy in OFFSETS
    ]
    homes = (q_hbm, k_hbm, v_hbm)

    def by_width(do):
        if not mixed:
            do(hi, hi)
            return

        @pl.when(wide)
        def _():
            do(hi, lo)

        @pl.when(jnp.logical_not(wide))
        def _():
            do(lo, hi)

    def columns(i):
        return pl.ds(pl.multiple_of(i * PACK, PACK), PACK)

    def wait_bytes(ref, sem):
        pltpu.make_async_copy(ref, ref, sem).wait()

    def wait_rows(count, sem):
        wait_bytes(tally.at[pl.ds(0, count)], sem)

    def load_own(i, a):
        slot = lax.rem(i, 3)
        pltpu.make_async_copy(
            homes[a].at[:, :, columns(i)], own.at[slot, a], own_sem.at[slot, a]
        ).start()

    def send_swap(i, a):
        slot, kept = lax.rem(i, 2), lax.rem(i, 3)
        wait_bytes(own.at[kept, a], own_sem.at[kept, a])
        if not raw:
            values = own[kept, a].reshape(SLOTS * CELLS, PACK)
            z_out[slot, a] = select(z_pack, values, z_pack_spans).astype(BF16)
        pltpu.make_async_remote_copy(
            src_ref=own.at[kept, a] if raw else z_out.at[slot, a],
            dst_ref=z_in.at[i, a],
            send_sem=z_send.at[i, a],
            recv_sem=z_recv.at[i, a],
            device_id={"dp": partner},
            device_id_type=MESH,
        ).start()

    def packed(values):
        taken = select(pack, values, pack_spans)
        parts = [taken[:, b * 128 : (b + 1) * 128].reshape(16, hi, 128) for b in range(2)]
        if mixed:
            parts = [p[:, :lo] for p in parts] + [p[:, lo:] for p in parts]
        return jnp.concatenate(parts, axis=1).astype(BF16)

    def send_grad(i):
        wait_bytes(grad.at[i], grad_sem.at[i])
        grad_out[i] = packed(grad[i].reshape(SLOTS * CELLS, PACK))

        def send(mine, other):
            for peer, alike in peers:
                at = pl.ds(0, 2 * (mine if alike else other))
                pltpu.make_async_remote_copy(
                    src_ref=grad_out.at[i, peer, at],
                    dst_ref=work.at[i, me, 3, at],
                    send_sem=gs_send.at[i],
                    recv_sem=f_recv.at[i],
                    device_id={"seq": peer},
                    device_id_type=MESH,
                ).start()

        by_width(send)
        work[i, me, 3] = grad_out[i, me]

    def send_array(i, a):
        slot, kept = lax.rem(i, 2), lax.rem(i, 3)
        wait_bytes(z_in.at[i, a], z_recv.at[i, a])

        @pl.when(i >= 2)
        def _():
            by_width(lambda mine, other: wait_rows(2 * (7 * mine + 8 * other), f_send.at[slot, a]))

        if not raw:
            arrived = select(z_unpack, z_in[i, a], z_unpack_spans).astype(BF16)
        for s in range(SLOTS):
            part = z_in[i, a, s] if raw else arrived[s * CELLS : (s + 1) * CELLS]
            moved[kept, a, s] = jnp.where(flags[s] == 1, part, own[kept, a, s])
        stage[slot, a] = packed(moved[kept, a].reshape(SLOTS * CELLS, PACK))

        def send(mine, other):
            for peer, alike in peers:
                at = pl.ds(0, 2 * (mine if alike else other))
                pltpu.make_async_remote_copy(
                    src_ref=stage.at[slot, a, peer, at],
                    dst_ref=work.at[i, me, a, at],
                    send_sem=f_send.at[slot, a],
                    recv_sem=f_recv.at[i],
                    device_id={"seq": peer},
                    device_id_type=MESH,
                ).start()

        by_width(send)
        work[i, me, a] = stage[slot, a, me]
        wait_bytes(z_in.at[i, a], z_send.at[i, a])

        @pl.when(i + 3 < CHUNKS)
        def _():
            load_own(i + 3, a)

        @pl.when(i + 2 < CHUNKS)
        def _():
            send_swap(i + 2, a)

    def time_chunk(i):
        by_width(lambda mine, other: wait_rows(15 * 8 * mine, f_recv.at[i]))

        def one(r, _):
            at = pl.ds(pl.multiple_of(r * 16, 16), 16)
            q, k, v, g = [work[i, :, a, at, :].reshape(256, 128) for a in range(4)]
            bias = diag_ref[...] + time_bias[pl.ds(r, 1), :]
            for a, value in enumerate(attend(q, k, v, g, bias)):
                work[i, :, a, at, :] = value.astype(BF16).reshape(16, 16, 128)
            return 0

        steps = jnp.where(wide, hi // 8, lo // 8) if mixed else hi // 8
        lax.fori_loop(0, steps, one, 0)

        def send(mine, other):
            at = pl.ds(0, 2 * mine)
            for peer, _ in peers:
                pltpu.make_async_remote_copy(
                    src_ref=work.at[i, peer, :, at],
                    dst_ref=back.at[i, me, :, at],
                    send_sem=b_send.at[i],
                    recv_sem=b_recv.at[i],
                    device_id={"seq": peer},
                    device_id_type=MESH,
                ).start()
            pltpu.make_async_copy(work.at[i, me, :, at], back.at[i, me, :, at], b_recv.at[i]).start()

        by_width(send)

    def space_chunk(i):
        kept = lax.rem(i, 3)

        def one(step, _):
            s, b = step // 2, lax.rem(step, 2)
            lanes = pl.ds(pl.multiple_of(b * 128, 128), 128)
            q, k, v = [moved[kept, a, s, :, lanes] for a in range(3)]
            seen = row_ref[s]
            g = grad[i, s, :, lanes] * seen
            o, dq, dk, dv = attend(q, k, v, g, space_bias[s, 0:1, :])
            o = o * seen.astype(F32)
            for a, value in enumerate((o, dq, dk, dv)):
                space[a, s, :, lanes] = value
            return 0

        lax.fori_loop(0, 2 * SLOTS, one, 0)
        wait_rows(64 * (lo + hi), b_recv.at[i])
        fetch = pltpu.make_async_copy(back.at[i], back_in, back_sem)
        fetch.start()
        fetch.wait()

        @pl.when(i > 0)
        def _():
            wait_bytes(result, out_sem)

        for a in range(4):
            value = back_in[:, a].astype(F32)
            if mixed:
                base = [value[:, b * lo : (b + 1) * lo] for b in range(2)]
                extra = value[:, 2 * lo :]
                device = lax.broadcasted_iota(jnp.int32, extra.shape, 0)
                extra = jnp.where(((device >> 2) + device) & 1 == 0, extra, 0.0)
                parts = [jnp.concatenate([base[b], extra[:, b * 8 : (b + 1) * 8]], 1) for b in range(2)]
            else:
                parts = [value[:, b * hi : (b + 1) * hi] for b in range(2)]
            parts = [p.reshape(cap, 128) for p in parts]
            taken = select(unpack, jnp.concatenate(parts, axis=1).astype(BF16), unpack_spans)
            summed = space[a].reshape(SLOTS * CELLS, PACK) + taken
            result[a] = summed.astype(BF16).reshape(SLOTS, CELLS, PACK)
        for a in range(4):
            pltpu.make_async_copy(result.at[a], out_hbm.at[a, :, :, columns(i)], out_sem).start()

    barrier = pltpu.get_barrier_semaphore()
    for peer, _ in peers:
        pl.semaphore_signal(barrier, inc=1, device_id={"seq": peer}, device_id_type=MESH)
    pl.semaphore_signal(barrier, inc=1, device_id={"dp": partner}, device_id_type=MESH)
    for i in range(3):
        for a in range(3):
            load_own(i, a)

    def load_grad(i, _):
        pltpu.make_async_copy(g_hbm.at[:, :, columns(i)], grad.at[i], grad_sem.at[i]).start()
        return 0

    lax.fori_loop(0, CHUNKS, load_grad, 0)

    flags = [flag_ref[lax.rem(group, 4) * 2 + s] for s in range(SLOTS)]

    def extents(ref):
        here = [ref[group * 2 + s] for s in range(SLOTS)]
        there = [ref[partner * 2 + s] for s in range(SLOTS)]
        return here, [jnp.where(flags[s] == 1, there[s], here[s]) for s in range(SLOTS)]

    home_counts, counts = extents(count_ref)
    home_rows, seen_rows = extents(rows_ref)
    home_cols, seen_cols = extents(cols_ref)
    areas = [seen_rows[s] * seen_cols[s] for s in range(SLOTS)]

    def places(index, extent_counts, extent_rows, extent_cols, first, second):
        later = index >= CELLS
        y, x = (index & (CELLS - 1)) >> 5, index & (GRID_W - 1)
        tall = jnp.where(later, extent_rows[1], extent_rows[0])
        broad = jnp.where(later, extent_cols[1], extent_cols[0])
        count = jnp.where(later, extent_counts[1], extent_counts[0])
        live = (y < tall) & (x < broad) & (me < count) & (jnp.where(later, second[1], first[1]) == 1)
        return jnp.where(live, jnp.where(later, second[0], first[0]) + y * broad + x, -1)

    across = lax.broadcasted_iota(jnp.int32, (1, SLOTS * CELLS), 1)
    along = lax.broadcasted_iota(jnp.int32, (SLOTS * CELLS, 1), 0)
    home_area = jnp.where(flags[0] == 1, home_rows[0] * home_cols[0], 256)
    target_area = jnp.where(flags[0] == 1, areas[0], 256)
    here = (counts, seen_rows, seen_cols)

    def one_hot(a, b):
        return jnp.where(a == b, 1.0, 0.0).astype(BF16)

    leaving = places(across, home_counts, home_rows, home_cols, (0, flags[0]), (home_area, flags[1]))
    pack[...] = one_hot(rank_col[...], places(across, *here, (0, 1), (areas[0], 1)))
    pl.semaphore_wait(barrier, 16)
    send_grad(0)
    if not raw:
        z_pack[...] = one_hot(lax.broadcasted_iota(jnp.int32, (z_cap, 1), 0), leaving)
    for a in range(3):
        send_swap(jnp.int32(0), a)
    send_grad(1)
    for a in range(3):
        send_swap(jnp.int32(1), a)

    def more_grads(i, _):
        send_grad(i)
        return 0

    lax.fori_loop(2, CHUNKS, more_grads, 0)
    arriving = places(along, *here, (0, flags[0]), (target_area, flags[1]))
    if not raw:
        z_unpack[...] = one_hot(arriving, lax.broadcasted_iota(jnp.int32, (1, z_cap), 1))
    landing = places(along, *here, (0, 1), (areas[0], 1))
    unpack[...] = one_hot(landing, rank_row[0:1, :])
    for s in range(SLOTS):
        part = landing[s * CELLS : (s + 1) * CELLS]
        row_ref[s] = jnp.broadcast_to(jnp.where(part >= 0, 1.0, 0.0), (CELLS, 128)).astype(BF16)
        cell = lax.broadcasted_iota(jnp.int32, (8, CELLS), 1)
        live = ((cell >> 5) < seen_rows[s]) & ((cell & (GRID_W - 1)) < seen_cols[s])
        space_bias[s] = jnp.where(live & (me < counts[s]), 0.0, MASKED)
    cell = cell_ref[...]
    rank = me * lo + cell + (hi - lo) * (2 * mx + (my + 1 - lax.rem(mx, 2)) // 2)
    count = jnp.where(rank < areas[0], counts[0], counts[1])
    count = jnp.where(rank < areas[0] + areas[1], count, FRAMES)
    frame = lax.broadcasted_iota(jnp.int32, cell.shape, 1) >> 4
    time_bias[...] = jnp.where(frame < count, 0.0, MASKED)
    first = lax.broadcasted_iota(jnp.int32, (256, 256), 0)
    second = lax.broadcasted_iota(jnp.int32, (256, 256), 1)
    diag_ref[...] = jnp.where((first & 15) == (second & 15), 0.0, MASKED)

    def done_by(u, times):
        return sum((u >= time).astype(jnp.int32) for time in times)

    def stage_of(u, times, do):
        def one(i, _):
            do(i)
            return 0

        lax.fori_loop(done_by(u - 1, times), done_by(u, times), one, 0)

    def step(i, _):
        for a in range(3):
            u = 3 * i + a

            @pl.when(i < CHUNKS)
            def _():
                send_array(i, a)

            stage_of(u, TIME_AT, time_chunk)
            stage_of(u, SPACE_AT, space_chunk)
        return 0

    lax.fori_loop(0, CHUNKS + 1, step, 0)
    wait_bytes(result, out_sem)

    def finish(i, _):
        def sent(mine, other):
            wait_rows(2 * (7 * mine + 8 * other), gs_send.at[i])
            wait_rows(15 * 8 * mine, b_send.at[i])

        by_width(sent)
        return 0

    lax.fori_loop(0, CHUNKS, finish, 0)
    for i in range(2):
        for a in range(3):
            by_width(lambda mine, other: wait_rows(2 * (7 * mine + 8 * other), f_send.at[i, a]))


def run_block(lo, hi, q, k, v, g, *tables):
    rows, cap, z_cap = 2 * hi, 16 * hi, 8 * (lo + hi)
    rank, cell_of = ranks(lo, hi)
    shape = (SLOTS, CELLS, WIDTH)
    pair = (SLOTS, CELLS, PACK)
    raw = hi == 64
    z_one = pair if raw else (z_cap, PACK)
    z_rows = 16 if raw else z_cap
    whole = pl.BlockSpec(memory_space=pl.ANY)
    local = pl.BlockSpec(memory_space=pltpu.VMEM)
    scalar = pl.BlockSpec(memory_space=pltpu.SMEM)
    dma = pltpu.SemaphoreType.DMA
    outs = pl.pallas_call(
        functools.partial(block_kernel, lo, hi),
        out_shape=[
            jax.ShapeDtypeStruct((4,) + shape, BF16),
            jax.ShapeDtypeStruct((CHUNKS, 16, 4, rows, 128), BF16),
            jax.ShapeDtypeStruct((128 * hi, 128), BF16),
        ],
        in_specs=[whole] * 4 + [scalar] * 4 + [local] * 3,
        out_specs=[whole] * 3,
        scratch_shapes=[
            pltpu.VMEM((3, 3) + pair, BF16),
            pltpu.VMEM((2, 3, z_rows, PACK), BF16),
            pltpu.VMEM((CHUNKS, 3) + z_one, BF16),
            pltpu.VMEM((3, 3) + pair, BF16),
            pltpu.VMEM((CHUNKS,) + pair, BF16),
            pltpu.VMEM((CHUNKS, 16, rows, 128), BF16),
            pltpu.VMEM((2, 3, 16, rows, 128), BF16),
            pltpu.VMEM((CHUNKS, 16, 4, rows, 128), BF16),
            pltpu.VMEM((16, 4, rows, 128), BF16),
            pltpu.VMEM((4,) + pair, F32),
            pltpu.VMEM((4,) + pair, BF16),
            pltpu.VMEM((cap, SLOTS * CELLS), BF16),
            pltpu.VMEM((SLOTS * CELLS, cap), BF16),
            pltpu.VMEM((z_rows, SLOTS * CELLS), BF16),
            pltpu.VMEM((SLOTS * CELLS, z_rows), BF16),
            pltpu.VMEM((SLOTS, CELLS, 128), BF16),
            pltpu.VMEM((SLOTS, 8, CELLS), F32),
            pltpu.VMEM((hi // 8, 256), F32),
            pltpu.VMEM((256, 256), F32),
            dma((CHUNKS, 3)),
            dma((CHUNKS, 3)),
            dma((3, 3)),
            dma((CHUNKS,)),
            dma((CHUNKS,)),
            dma((2, 3)),
            dma((CHUNKS,)),
            dma((CHUNKS,)),
            dma((CHUNKS,)),
            dma,
            dma,
        ],
        compiler_params=pltpu.CompilerParams(
            collective_id=(lo + hi) // 8, has_side_effects=True, vmem_limit_bytes=63 * 2**20
        ),
        cost_estimate=pl.CostEstimate(
            flops=4 * 10**10, bytes_accessed=48 * 2**20, transcendentals=10**7
        ),
    )(
        *[value.reshape(shape) for value in (q, k, v, g)],
        *tables,
        rank.reshape(cap, 1),
        np.tile(rank, (8, 1)),
        cell_of,
    )
    return outs[0].reshape(4, SLOTS, 1, CELLS, WIDTH)


SIZES = ((48, 48), (56, 56), (64, 64))


def shards(q, k, v, g, frame_counts, patch_rows, patch_cols, swap_flags):
    flags = jnp.concatenate([swap_flags, swap_flags]).reshape(16)
    areas = patch_rows * patch_cols
    areas = jnp.where(flags == 1, jnp.roll(areas, 8), areas)
    needed = jnp.max(jnp.sum(areas.reshape(8, SLOTS), axis=1))
    args = (q, k, v, g, frame_counts, patch_rows, patch_cols, swap_flags.reshape(8))
    if len(SIZES) == 1:
        done = run_block(*SIZES[0], *args)
        return tuple(done[a] for a in range(4))
    choice = sum((needed > 8 * (lo + hi)).astype(jnp.int32) for lo, hi in SIZES[:-1])
    done = lax.switch(choice, [functools.partial(run_block, lo, hi) for lo, hi in SIZES], *args)
    return tuple(done[a] for a in range(4))


def solution(mesh):
    rows = P("dp", "seq", None, None)
    return jax.shard_map(
        shards,
        mesh=mesh,
        in_specs=(rows, rows, rows, rows, P(), P(), P(), P()),
        out_specs=(rows, rows, rows, rows),
        check_vma=False,
    )
```

time: 351 us -> 300 us (0.85)
  the two profiles are of different devices: /device:TPU:36 before, /device:TPU:50 now
where the time goes in v2:
time: 300 us; the launch traced here: 295 us
  Pallas kernels  266 us (89%)
  loops' own time  14.1 us (5%)
  local copies, waits for them, and re-layouts  10.4 us (3%)
    pallas_call x1, Pallas kernels, run_block(): pl.pallas_call(functools.partial(block_kernel, lo, hi), out_shape=[jax.Sh...  266 us
    another operation x1, loops' own time, shards(): lax.switch(choice, [functools.partial(run_block, lo, hi) for lo, hi in SI...  14.1 us
    squeeze x1, local copies, waits for them, and re-layouts, shards(): return tuple((done[a] for a in range(4)))  9.22 us

profile of v2, /device:TPU:50, one launch (start us, length us, event | category | flops | bytes accessed | tf_op | source)
XLA Modules:
  0.0 295.5 jit_solution(5965536287503167289)
XLA Ops:
  0.6 0.7 mul.3
  1.3 0.8 add_compare_fusion
  2.1 0.1 copy.53
  2.2 0.1 eq.7
  2.3 0.1 fusion
  2.4 0.1 add_select_fusion
  2.5 0.8 copy.54
  3.2 0.1 reshape.66
  3.3 0.1 reshape.65
  3.4 0.1 reduce_sum.9
  3.5 0.6 reduce_max.9
  5.5 280.5 %conditional.1 = (bf16[4,2,512,1536]{3,2,1,0:T(8,128)(2,1)}) conditional(s32[]{:T(128)} %clamp.3, (bf16[2,1,512,1536]{3,2,1,0:T(8,128)(2,1)}, bf16[2,1,512,1536]{3,2,1,0:T(8,128)(2,1)}, bf16[2,1,512,1536]{3,2,1,0:T(8,128)(2,1)}, bf16[2,1,512,1536]{3,2,1,0:T(8,128)(2,1)}, s32[16]{0:T(128)}, /*index=5*/s32[16]{0:T(128)}, ...), branch_computations={%region_2.3_spmd.clone, %region_3.4_spmd.clone, %region_4.5_spmd.c... | conditional | flops 40000000000 | bytes 50331656 | solution.py:519
  10.4 266.4 %branch_1_fun.1 = (bf16[4,2,512,1536]{3,2,1,0:T(8,128)(2,1)}, bf16[6,16,4,112,128]{4,3,2,1,0:T(8,128)(2,1)}, bf16[7168,128]{1,0:T(8,128)(2,1)}) custom-call(bf16[2,512,1536]{2,1,0:T(8,128)(2,1)} %bitcast.33, bf16[2,512,1536]{2,1,0:T(8,128)(2,1)} %bitcast.36, bf16[2,512,1536]{2,1,0:T(8,128)(2,1)} %bitcast.39, bf16[2,512,1536]{2,1,0:T(8,128)(2,1)} %bitcast.42, ...), custom_call_target="tpu_custom_call" | custom-call | flops 40000000000 | bytes 50331648 | tf_op jit(solution)/shard_map/cond/branch_1_fun/pallas_call | solution.py:449
  285.9 9.2 %slice_bitcast_fusion = (bf16[2,1,512,1536]{3,2,1,0:T(8,128)(2,1)}, bf16[2,1,512,1536]{3,2,1,0:T(8,128)(2,1)}, bf16[2,1,512,1536]{3,2,1,0:T(8,128)(2,1)}, bf16[2,1,512,1536]{3,2,1,0:T(8,128)(2,1)}) fusion(bf16[4,2,512,1536]{3,2,1,0:T(8,128)(2,1)} %get-tuple-element.234), kind=kLoop, calls=%fused_computation | loop fusion | bytes 25165824 | tf_op jit(solution)/shard_map/squeeze | solution.py:520
